TPU v7x, 512 devices: a whole 4x8x8 slice. The times are simulated.
512 devices in a mesh: rad: 32 (over z_hi, x, core), lat: 16 (over z_lo, y).
Axes of the slice: x: 4, y: 8, z: 8 (z_hi: 4, z_lo: 2; z = z_hi * 2 + z_lo), core: 2. Of those that a mesh axis runs over, the one named last changes fastest.
Arguments:
- nonlinear_samples: bfloat16 [32, 2, 1536, 3072], P('rad', None, 'lat'), may hold values from -6 to 6
- legendre: bfloat16 [256, 1536, 1024], P('rad', 'lat'), may hold values from -0.21875 to 0.21875
- assign: int32 [256], replicated, may hold values from 0 to 255, each once
- counts: int32 [256], replicated, may hold values from 513 to 1024, as said below
- spectral_state: float32 [1024, 256, 128], P('lat', 'rad'), may hold values from -6 to 6
- inverses: float32 [1024, 4, 8, 8], P('lat'), may hold values from -1 to 1
Outputs:
- advanced: float32 [1024, 256, 128], P('lat', 'rad')
Inputs may be any that keep to these rules, and one draw needn't show every extreme that they name: Slot s carries order assign[s]; each order 0 to 255 stands in exactly one slot. counts[m] is at most 1024 - m, and order 0 has 1024 live degrees.
All inputs are finite; a program needn't handle non-finite values.
Results may differ from a plain program's by a relative error of at most 0.0034.
Values may be sent and summed in bfloat16 or wider, within the bound.
A program may use at most 64 MiB of HBM per device.

v0:
```python
import math
import jax
import jax.numpy as jnp
from jax import lax
from jax.sharding import PartitionSpec as P


def trig_table(assign, lon_count):
    longitude = jnp.arange(lon_count, dtype=jnp.int32)
    phases = longitude[:, None] * assign[None, :] % lon_count
    angles = phases.astype(jnp.float32) * (2.0 * math.pi / lon_count)
    normalizing_multiplier = 1.0 / math.sqrt(lon_count)
    cosine = (jnp.cos(angles) * normalizing_multiplier).astype(jnp.bfloat16)
    sine = (-jnp.sin(angles) * normalizing_multiplier).astype(jnp.bfloat16)
    return jnp.stack([cosine, sine], axis=2).reshape(lon_count, 2 * assign.shape[0])


def radial_step(spectral_state, source, inverses, degree):
    deg_rows, slot_count, width = spectral_state.shape
    shell_number = width // 4
    blk_size = inverses.shape[2]
    blk_count = shell_number // blk_size
    field_now = spectral_state.reshape(deg_rows, slot_count, 4, shell_number)
    zero_rim = jnp.zeros((deg_rows, slot_count, 4, 1), jnp.float32)
    outward = jnp.concatenate([field_now[..., 1:], zero_rim], axis=3)
    inward = jnp.concatenate([zero_rim, field_now[..., :-1]], axis=3)
    radial_spacing = 0.65 / (shell_number + 1)
    radius = 0.35 + 0.65 * (jnp.arange(shell_number, dtype=jnp.float32) + 1.0) / (shell_number + 1)
    ratios = radial_spacing / radius
    degree_term = degree[:, None, None, None] * (degree[:, None, None, None] + 1.0)
    central = 0.5 * radial_spacing * radial_spacing * degree_term / (radius * radius)
    right_side = (
        field_now + 0.5 * (outward - 2.0 * field_now + inward) + 0.5 * ratios * (outward - inward)
    )
    right_side = (
        right_side - central * field_now + source.reshape(deg_rows, slot_count, 4, shell_number)
    )
    lower_link = -0.5 * (1.0 - ratios[0::blk_size])
    upper_link = -0.5 * (1.0 + ratios[blk_size - 1 :: blk_size])
    blocks = jnp.moveaxis(right_side.reshape(deg_rows, slot_count, 4, blk_count, blk_size), 3, 0)
    block_inverse = jnp.moveaxis(inverses, 1, 0)
    first_unit = (jnp.arange(blk_size, dtype=jnp.int32) == 0).astype(jnp.float32)
    start_carry = jnp.zeros((deg_rows, slot_count, 4), jnp.float32)

    def forward(carried, items):
        matrix, block, link = items
        block = block - link * carried[..., None] * first_unit
        result = jnp.einsum("lij,locj->loci", matrix, block, precision=lax.Precision.HIGHEST)
        return (result[..., blk_size - 1], result)

    def inverse_sweep(carried, items):
        matrix, partial_solution, link = items
        result = (
            partial_solution - link * carried[..., None] * matrix[:, None, None, :, blk_size - 1]
        )
        return (result[..., 0], result)

    _, forward_blocks = lax.scan(forward, start_carry, (block_inverse, blocks, lower_link))
    _, solved = lax.scan(
        inverse_sweep, start_carry, (block_inverse, forward_blocks, upper_link), reverse=True
    )
    return jnp.moveaxis(solved, 0, 3).reshape(deg_rows, slot_count, 4 * shell_number)


def body(nonlinear_samples, legendre, assign, counts, spectral_state, inverses):
    rad_local = nonlinear_samples.shape[0]
    lat_local = nonlinear_samples.shape[2]
    lon_count = nonlinear_samples.shape[3]
    order_total = assign.shape[0]
    order_local = legendre.shape[0]
    degree_local = spectral_state.shape[0]
    shell_grand_number = spectral_state.shape[2] // 4
    table = trig_table(assign, lon_count)
    flat_rows = nonlinear_samples.reshape(rad_local * 2 * lat_local, lon_count)
    fourier_modes = jnp.dot(flat_rows, table, preferred_element_type=jnp.float32).astype(
        jnp.bfloat16
    )
    fourier_modes = fourier_modes.reshape(rad_local, 2, lat_local, order_total, 2)
    thermal_part = lax.all_to_all(
        fourier_modes[:, 0], "rad", split_axis=2, concat_axis=0, tiled=True
    )
    magnetic_potential_part = lax.all_to_all(
        fourier_modes[:, 1], "rad", split_axis=2, concat_axis=0, tiled=True
    )
    permuted_dims = jnp.stack([thermal_part, magnetic_potential_part], axis=1)
    columns = lax.all_to_all(legendre, "lat", split_axis=2, concat_axis=1, tiled=True)
    whole = lax.all_gather(permuted_dims, "lat", axis=2, tiled=True)
    band_total = lax.axis_size("lat")
    legendre_table_bands = columns.reshape(order_local, band_total, lat_local, degree_local)
    value_bands = whole.reshape(shell_grand_number, 2, band_total, lat_local, order_local, 2)
    partial_value = jnp.einsum(
        "obtl,rfbtok->blofkr", legendre_table_bands, value_bands, preferred_element_type=jnp.float32
    )
    partial_value = lax.optimization_barrier(partial_value.astype(jnp.bfloat16)).astype(jnp.float32)
    summed = jnp.sum(partial_value, axis=0).reshape(
        degree_local, order_local, 4 * shell_grand_number
    )
    rad_position = lax.axis_index("rad")
    lat_position = lax.axis_index("lat")
    my_orders = lax.dynamic_slice_in_dim(assign, rad_position * order_local, order_local, 0)
    order_ids = jnp.arange(order_total, dtype=jnp.int32)
    my_counts = jnp.sum(
        jnp.where(my_orders[:, None] == order_ids[None, :], counts[None, :], 0), axis=1
    )
    degree_ids = lat_position * degree_local + jnp.arange(degree_local, dtype=jnp.int32)
    limits = my_orders + my_counts
    live = (degree_ids[:, None] >= my_orders[None, :]) & (degree_ids[:, None] < limits[None, :])
    source = jnp.where(live[:, :, None], summed, jnp.zeros_like(summed))
    return radial_step(spectral_state, source, inverses, degree_ids.astype(jnp.float32))


def solution(mesh):
    return jax.shard_map(
        body,
        mesh=mesh,
        in_specs=(
            P("rad", None, "lat", None),
            P("rad", "lat", None),
            P(),
            P(),
            P("lat", "rad", None),
            P("lat", None, None, None),
        ),
        out_specs=P("lat", "rad", None),
        check_vma=False,
    )
```

profile of v0, /device:TPU:1, one launch (start us, length us, event | category | flops | bytes accessed | tf_op | source)
XLA Modules:
  0.0 378.4 jit_solution(9484199052676013640)
XLA Ops:
  6.5 14.2 %multiply_convert_fusion.1 = (bf16[3072,256,1]{1,0,2:T(8,128)(2,1)S(1)}, bf16[3072,256,1]{1,0,2:T(8,128)(2,1)S(1)}) fusion(s32[256]{0:T(256)} %param.12), kind=kLoop, calls=%fused_computation.29 | loop fusion | flops 11010048 | bytes 3146752 | tf_op jit(solution)/shard_map/convert_element_type | solution.py:13
  20.7 1.9 pad_maximum_fusion
  22.7 8.8 %copy.108 = bf16[3072,256,2]{0,2,1:T(2,128)(2,1)} copy(bf16[3072,256,2]{1,0,2:T(8,128)(2,1)} %pad_maximum_fusion) | data formatting | bytes 6291456 | tf_op jit(solution)/shard_map/stack | solution.py:15
  31.4 7.5 %reshape.244 = bf16[3072,512]{0,1:T(8,128)(2,1)} reshape(bf16[3072,256,2]{0,2,1:T(2,128)(2,1)} %copy.108) | data formatting | bytes 6291456 | tf_op jit(solution)/shard_map/reshape | solution.py:15
  38.9 3.1 fusion.20
  42.9 0.8 copy.114
  43.6 14.4 %all-to-all-start.1 = ((bf16[1,96,256,2]{1,3,0,2:T(2,128)(2,1)}), bf16[1,96,256,2]{1,3,0,2:T(2,128)(2,1)S(1)}, u32[]{:S(2)}, u32[]{:S(2)}) async-start(bf16[1,96,256,2]{1,3,0,2:T(2,128)(2,1)} %copy.114), calls=%async_computation.1 | async-start | bytes 262144 | tf_op jit(solution)/shard_map/all_to_all | solution.py:82
  58.2 0.8 copy.111
  59.0 10.4 %all-to-all-done.1 = bf16[1,96,256,2]{1,3,0,2:T(2,128)(2,1)S(1)} async-done(((bf16[1,96,256,2]{1,3,0,2:T(2,128)(2,1)}), bf16[1,96,256,2]{1,3,0,2:T(2,128)(2,1)S(1)}, u32[]{:S(2)}, u32[]{:S(2)}) %all-to-all-start.1) | async-done | bytes 98336 | tf_op jit(solution)/shard_map/all_to_all | solution.py:82
  69.4 3.7 all-to-all-start
  73.2 11.1 %all-to-all-done = bf16[1,96,256,2]{1,3,0,2:T(2,128)(2,1)S(1)} async-done(((bf16[1,96,256,2]{1,3,0,2:T(2,128)(2,1)}), bf16[1,96,256,2]{1,3,0,2:T(2,128)(2,1)S(1)}, u32[]{:S(2)}, u32[]{:S(2)}) %all-to-all-start) | async-done | bytes 98336 | tf_op jit(solution)/shard_map/all_to_all | solution.py:79
  84.3 2.2 copy.116
  86.6 2.9 copy.118
  89.5 7.4 %all-to-all-start.2 = ((bf16[8,96,1024]{1,0,2:T(8,128)(2,1)}), bf16[8,96,1024]{1,0,2:T(8,128)(2,1)}, u32[]{:S(2)}, u32[]{:S(2)}) async-start(bf16[8,96,1024]{1,0,2:T(8,128)(2,1)} %copy.118), calls=%async_computation.2 | async-start | bytes 4194304 | tf_op jit(solution)/shard_map/all_to_all | solution.py:86
  97.4 1.3 copy.122
  99.3 70.4 %all-to-all-done.2 = bf16[8,96,1024]{1,0,2:T(8,128)(2,1)} async-done(((bf16[8,96,1024]{1,0,2:T(8,128)(2,1)}), bf16[8,96,1024]{1,0,2:T(8,128)(2,1)}, u32[]{:S(2)}, u32[]{:S(2)}) %all-to-all-start.2) | async-done | bytes 1572896 | tf_op jit(solution)/shard_map/all_to_all | solution.py:86
  169.7 102.0 %all-gather.2.cloned.1.call-done = bf16[32,2,1536,8,2]{0,3,4,1,2:T(8,128)(2,1)} async-done(((bf16[32,2,96,8,2]{0,3,4,1,2:T(8,128)(2,1)}), bf16[32,2,1536,8,2]{0,3,4,1,2:T(8,128)(2,1)}) %all-gather.2.cloned.1.call-update) | async-done | bytes 3145744 | tf_op jit(solution)/shard_map/all_gather | solution.py:87
  271.8 8.7 %convert_bitcast_fusion = bf16[16,64,8,2,2,32]{1,5,4,3,2,0:T(8,128)(2,1)S(1)} fusion(bf16[32,2,16,96,8,2]{0,4,5,1,3,2:T(8,128)(2,1)} %bitcast.114, bf16[8,96,16,64]{1,0,3,2:T(8,128)(2,1)} %bitcast.15), kind=kOutput, calls=%fused_computation.24 | convolution fusion | flops 202375168 | bytes 6815744 | tf_op jit(solution)/shard_map/obtl,rfbtok->blofkr/dot_general | solution.py:91
  280.5 1.0 convert_reduce_fusion
  281.4 1.1 add_bitcast_fusion
  282.5 0.9 broadcast.271.clone2
  283.4 77.8 %while.30 = (s32[]{:T(128)}, f32[64,8,4]{1,2,0:T(4,128)S(1)}, f32[4,64,8,4,8]{1,4,3,2,0:T(8,128)}, f32[4,64,8,4,8]{1,4,0,3,2:T(8,128)}, f32[4]{0:T(128)S(1)}, /*index=5*/f32[4,64,8,8]{3,2,1,0:T(8,128)}, s32[]{:T(128)}) while((s32[]{:T(128)}, f32[64,8,4]{1,2,0:T(4,128)S(1)}, f32[4,64,8,4,8]{1,4,3,2,0:T(8,128)}, ...), condition=%wide.region_3.4_spmd.clone, body=%wide.region_2.3_spmd.clone.sunk | while | flops 1607698 | bytes 1025185 | solution.py:58
  283.4 0.9 constant_dynamic-slice_fusion.5
  284.4 0.9 copy.162
  286.5 14.9 %fusion.30 = f32[64,8,4,8]{1,3,2,0:T(8,128)S(1)} fusion(f32[1,64,8,4,8]{4,2,3,1,0:T(8,128)S(1)} %copy.162, f32[8]{0:T(128)S(1)} %compare_convert_fusion.2, f32[64,8,4]{1,2,0:T(4,128)S(1)} %bitcast.101, f32[4,64,8,8]{3,2,1,0:T(8,128)} %get-tuple-element.387, s32[]{:T(128)} %get-tuple-element.375), kind=kOutput, calls=%fused_computation.9.clone.1 | convolution fusion | flops 1605632 | bytes 401952 | tf_op jit(solution)/shard_map/while/body/eval_jaxpr/lij,locj->loci/dot_general | solution.py:48
  302.1 0.7 constant_dynamic-update-slice_fusion.2
  302.9 0.9 constant_dynamic-slice_fusion.5
  303.8 0.9 copy.162
  306.0 14.9 %fusion.30 = f32[64,8,4,8]{1,3,2,0:T(8,128)S(1)} fusion(f32[1,64,8,4,8]{4,2,3,1,0:T(8,128)S(1)} %copy.162, f32[8]{0:T(128)S(1)} %compare_convert_fusion.2, f32[64,8,4]{1,2,0:T(4,128)S(1)} %bitcast.101, f32[4,64,8,8]{3,2,1,0:T(8,128)} %get-tuple-element.387, s32[]{:T(128)} %get-tuple-element.375), kind=kOutput, calls=%fused_computation.9.clone.1 | convolution fusion | flops 1605632 | bytes 401952 | tf_op jit(solution)/shard_map/while/body/eval_jaxpr/lij,locj->loci/dot_general | solution.py:48
  321.5 0.7 constant_dynamic-update-slice_fusion.2
  322.3 0.9 constant_dynamic-slice_fusion.5
  323.3 0.9 copy.162
  325.4 14.9 %fusion.30 = f32[64,8,4,8]{1,3,2,0:T(8,128)S(1)} fusion(f32[1,64,8,4,8]{4,2,3,1,0:T(8,128)S(1)} %copy.162, f32[8]{0:T(128)S(1)} %compare_convert_fusion.2, f32[64,8,4]{1,2,0:T(4,128)S(1)} %bitcast.101, f32[4,64,8,8]{3,2,1,0:T(8,128)} %get-tuple-element.387, s32[]{:T(128)} %get-tuple-element.375), kind=kOutput, calls=%fused_computation.9.clone.1 | convolution fusion | flops 1605632 | bytes 401952 | tf_op jit(solution)/shard_map/while/body/eval_jaxpr/lij,locj->loci/dot_general | solution.py:48
  341.0 0.7 constant_dynamic-update-slice_fusion.2
  341.8 0.9 constant_dynamic-slice_fusion.5
  342.7 0.9 copy.162
  344.9 14.9 %fusion.30 = f32[64,8,4,8]{1,3,2,0:T(8,128)S(1)} fusion(f32[1,64,8,4,8]{4,2,3,1,0:T(8,128)S(1)} %copy.162, f32[8]{0:T(128)S(1)} %compare_convert_fusion.2, f32[64,8,4]{1,2,0:T(4,128)S(1)} %bitcast.101, f32[4,64,8,8]{3,2,1,0:T(8,128)} %get-tuple-element.387, s32[]{:T(128)} %get-tuple-element.375), kind=kOutput, calls=%fused_computation.9.clone.1 | convolution fusion | flops 1605632 | bytes 401952 | tf_op jit(solution)/shard_map/while/body/eval_jaxpr/lij,locj->loci/dot_general | solution.py:48
  360.4 0.7 constant_dynamic-update-slice_fusion.2
  361.3 9.2 %while.29 = (s32[]{:T(128)}, f32[64,8,4]{0,2,1:T(4,128)S(1)}, f32[4,64,8,4,8]{1,4,3,2,0:T(8,128)S(1)}, f32[4,64,8,4,8]{1,4,3,2,0:T(8,128)}, f32[4]{0:T(128)S(1)}...) while((s32[]{:T(128)}, f32[64,8,4]{0,2,1:T(4,128)S(1)}, f32[4,64,8,4,8]{1,4,3,2,0:T(8,128)S(1)}, ...), condition=%wide.region_5.6_spmd, body=%wide.region_4.5_spmd.sunk | while | flops 38915 | bytes 459641 | solution.py:59
  361.4 0.7 dynamic_slice.63
  362.6 0.9 subtract_dynamic-update-slice_fusion.2
  363.7 0.7 dynamic_slice.63
  364.9 0.9 subtract_dynamic-update-slice_fusion.2
  366.0 0.7 dynamic_slice.63
  367.3 0.9 subtract_dynamic-update-slice_fusion.2
  368.3 0.7 dynamic_slice.63
  369.6 0.9 subtract_dynamic-update-slice_fusion.2
  370.6 0.9 copy.129
  (86 shorter events, 12.9 us)
Async XLA Ops:
  6.5 32.4 %copy-start = (bf16[1,2,96,3072]{3,2,1,0:T(8,128)(2,1)S(1)}, bf16[1,2,96,3072]{3,2,1,0:T(8,128)(2,1)}, u32[]{:S(2)}) copy-start(bf16[1,2,96,3072]{3,2,1,0:T(8,128)(2,1)} %param.10) | copy-start | bytes 3538948
  42.2 44.4 %copy-start.1 = (bf16[8,96,1024]{2,1,0:T(8,128)(2,1)S(1)}, bf16[8,96,1024]{2,1,0:T(8,128)(2,1)}, u32[]{:S(2)}) copy-start(bf16[8,96,1024]{2,1,0:T(8,128)(2,1)} %param.11) | copy-start | bytes 4718596
  43.6 25.8 %all-to-all-start.1 = ((bf16[1,96,256,2]{1,3,0,2:T(2,128)(2,1)}), bf16[1,96,256,2]{1,3,0,2:T(2,128)(2,1)S(1)}, u32[]{:S(2)}, u32[]{:S(2)}) async-start(bf16[1,96,256,2]{1,3,0,2:T(2,128)(2,1)} %copy.114), calls=%async_computation.1 | async-start | bytes 262144 | tf_op jit(solution)/shard_map/all_to_all | solution.py:82
  69.4 14.8 %all-to-all-start = ((bf16[1,96,256,2]{1,3,0,2:T(2,128)(2,1)}), bf16[1,96,256,2]{1,3,0,2:T(2,128)(2,1)S(1)}, u32[]{:S(2)}, u32[]{:S(2)}) async-start(bf16[1,96,256,2]{1,3,0,2:T(2,128)(2,1)} %copy.111), calls=%async_computation | async-start | bytes 262144 | tf_op jit(solution)/shard_map/all_to_all | solution.py:79
  73.1 198.7 %all-gather.2.cloned.1.call-start = ((), (), s32[]{:S(2)}) async-start(), calls=%async_computation.3 | async-start | bytes 13369344 | tf_op jit(solution)/shard_map/all_gather | solution.py:87
  86.5 10.5 %copy-start.4 = (s32[256]{0:T(256)S(1)}, s32[256]{0:T(256)}, u32[]{:S(2)}) copy-start(s32[256]{0:T(256)} %param.12) | copy-start | bytes 3076
  86.6 10.6 %copy-start.3 = (f32[64,8,128]{2,1,0:T(8,128)S(1)}, f32[64,8,128]{2,1,0:T(8,128)}, u32[]{:S(2)}) copy-start(f32[64,8,128]{2,1,0:T(8,128)} %param.14) | copy-start | bytes 786436
  89.4 7.9 %copy-start.2 = (f32[64,4,8,8]{0,3,2,1:T(8,128)S(1)}, f32[64,4,8,8]{0,3,2,1:T(8,128)}, u32[]{:S(2)}) copy-start(f32[64,4,8,8]{0,3,2,1:T(8,128)} %param.15) | copy-start | bytes 196612
  89.5 9.3 %copy-start.5 = (s32[256]{0:T(256)S(1)}, s32[256]{0:T(256)}, u32[]{:S(2)}) copy-start(s32[256]{0:T(256)} %param.13) | copy-start | bytes 3076
  89.5 80.3 %all-to-all-start.2 = ((bf16[8,96,1024]{1,0,2:T(8,128)(2,1)}), bf16[8,96,1024]{1,0,2:T(8,128)(2,1)}, u32[]{:S(2)}, u32[]{:S(2)}) async-start(bf16[8,96,1024]{1,0,2:T(8,128)(2,1)} %copy.118), calls=%async_computation.2 | async-start | bytes 4194304 | tf_op jit(solution)/shard_map/all_to_all | solution.py:86
Sparse Core Ops, SparseCore 0:
  86.7 185.0 all-gather.1
where the time goes:
time: 379 us; the launch traced here: 378 us
  waiting for transfers between devices  194 us (51%)
  matrix products  71.3 us (19%)
  local copies, waits for them, and re-layouts  45.8 us (12%)
  other arithmetic  27.6 us (7%)
  starting transfers between devices  25.5 us (7%)
  between operations  13.6 us (4%)
    all_gather x1, waiting for transfers between devices, body(): whole = lax.all_gather(permuted_dims, 'lat', axis=2, tiled=True)  102 us
    all_to_all x1, waiting for transfers between devices, body(): lax.all_to_all(legendre, 'lat', split_axis=2, concat_axis=1, tiled=True)  70.4 us
    dot_general x4, matrix products, forward(): jnp.einsum('lij,locj->loci', matrix, block, precision=lax.Precision.HIGHEST)  59.6 us
    all_to_all x1, starting transfers between devices, body(): lax.all_to_all(fourier_modes[:, 1], 'rad', split_axis=2, concat_axis=0, t...  14.4 us
    convert_element_type x1, other arithmetic, trig_table(): cosine = (jnp.cos(angles) * normalizing_multiplier).astype(jnp.bfloat16)  14.2 us
    dynamic_slice x24, local copies, waits for them, and re-layouts, radial_step(): lax.scan(forward, start_carry, (block_inverse, blocks, lower_link))  12.4 us
    all_to_all x1, waiting for transfers between devices, body(): lax.all_to_all(fourier_modes[:, 0], 'rad', split_axis=2, concat_axis=0, t...  11.1 us
    all_to_all x1, waiting for transfers between devices, body(): lax.all_to_all(fourier_modes[:, 1], 'rad', split_axis=2, concat_axis=0, t...  10.4 us
  transfers between devices with their start and end apart: 4, of which 4 were waited for; matrix products, arithmetic and copies ran while one was open for 2% of the time, Pallas kernels for 0%

commit v1 on v0

--- a/solution.py
+++ b/solution.py
@@ -84,7 +84,12 @@
     )
     permuted_dims = jnp.stack([thermal_part, magnetic_potential_part], axis=1)
     columns = lax.all_to_all(legendre, "lat", split_axis=2, concat_axis=1, tiled=True)
-    whole = lax.all_gather(permuted_dims, "lat", axis=2, tiled=True)
+    whole = jnp.concatenate(
+        lax.all_to_all(
+            jnp.stack([permuted_dims for _ in range(lax.axis_size("lat"))], 0), "lat", 0, 0
+        ),
+        2,
+    )
     band_total = lax.axis_size("lat")
     legendre_table_bands = columns.reshape(order_local, band_total, lat_local, degree_local)
     value_bands = whole.reshape(shell_grand_number, 2, band_total, lat_local, order_local, 2)

time: 379 us -> 336 us (0.89)
  waiting for transfers between devices: 194 us -> 155 us
  between operations: 13.6 us -> 0.25 us
  starting transfers between devices: 25.5 us -> 32 us
  local copies, waits for them, and re-layouts: 45.8 us -> 51.2 us
  matrix products: 71.3 us -> 66.2 us
    all_gather x1 -> x0, waiting for transfers between devices: 102 us -> none  [body(): whole = lax.all_gather(permuted_dims, 'lat', axis=2, tiled=True)]
    all_to_all x0 -> x1, waiting for transfers between devices: none -> 88.2 us  [body(): lax.all_to_all(jnp.stack([permuted_dims for _ in range(lax.axis_size('lat...]
    all_to_all x1, waiting for transfers between devices: 70.4 us -> 48.4 us  [body(): lax.all_to_all(legendre, 'lat', split_axis=2, concat_axis=1, tiled=True)]
    all_to_all x0 -> x1, starting transfers between devices: none -> 6.67 us  [body(): lax.all_to_all(jnp.stack([permuted_dims for _ in range(lax.axis_size('lat...]
    dot_general x1, matrix products: 8.66 us -> 3.43 us  [body(): jnp.einsum('obtl,rfbtok->blofkr', legendre_table_bands, value_bands, pref...]
  transfers between devices with their start and end apart: 4 -> 4, of which waited for: 4 -> 4; matrix products, arithmetic and copies ran while one was open for 2% -> 3% of each run, Pallas kernels for 0% -> 0%
where the time goes in v1:
time: 336 us; the launch traced here: 333 us
  waiting for transfers between devices  155 us (46%)
  matrix products  66.2 us (20%)
  local copies, waits for them, and re-layouts  51.2 us (15%)
  starting transfers between devices  32 us (10%)
  other arithmetic  27.6 us (8%)
    all_to_all x1, waiting for transfers between devices, body(): lax.all_to_all(jnp.stack([permuted_dims for _ in range(lax.axis_size('lat...  88.2 us
    dot_general x4, matrix products, forward(): jnp.einsum('lij,locj->loci', matrix, block, precision=lax.Precision.HIGHEST)  59.6 us
    all_to_all x1, waiting for transfers between devices, body(): lax.all_to_all(legendre, 'lat', split_axis=2, concat_axis=1, tiled=True)  48.4 us
    all_to_all x1, starting transfers between devices, body(): lax.all_to_all(fourier_modes[:, 1], 'rad', split_axis=2, concat_axis=0, t...  14.4 us
    convert_element_type x1, other arithmetic, trig_table(): cosine = (jnp.cos(angles) * normalizing_multiplier).astype(jnp.bfloat16)  14.2 us
    dynamic_slice x24, local copies, waits for them, and re-layouts, radial_step(): lax.scan(forward, start_carry, (block_inverse, blocks, lower_link))  12.4 us
    all_to_all x1, waiting for transfers between devices, body(): lax.all_to_all(fourier_modes[:, 1], 'rad', split_axis=2, concat_axis=0, t...  10.4 us
    another operation x1, local copies, waits for them, and re-layouts, trig_table(): jnp.stack([cosine, sine], axis=2).reshape(lon_count, 2 * assign.shape[0])  8.78 us
  transfers between devices with their start and end apart: 4, of which 4 were waited for; matrix products, arithmetic and copies ran while one was open for 3% of the time, Pallas kernels for 0%

profile of v1, /device:TPU:1, one launch (start us, length us, event | category | flops | bytes accessed | tf_op | source)
XLA Modules:
  0.0 333.2 jit_solution(13857959219880809567)
XLA Ops:
  0.0 14.2 %multiply_convert_fusion.1 = (bf16[3072,256,1]{1,0,2:T(8,128)(2,1)S(1)}, bf16[3072,256,1]{1,0,2:T(8,128)(2,1)S(1)}) fusion(s32[256]{0:T(256)} %param.12), kind=kLoop, calls=%fused_computation.29 | loop fusion | flops 11010048 | bytes 3146752 | tf_op jit(solution)/shard_map/convert_element_type | solution.py:13
  14.2 2.0 pad_maximum_fusion
  16.1 8.8 %copy.103 = bf16[3072,256,2]{0,2,1:T(2,128)(2,1)} copy(bf16[3072,256,2]{1,0,2:T(8,128)(2,1)} %pad_maximum_fusion) | data formatting | bytes 6291456 | tf_op jit(solution)/shard_map/stack | solution.py:15
  24.9 7.5 %reshape.246 = bf16[3072,512]{0,1:T(8,128)(2,1)} reshape(bf16[3072,256,2]{0,2,1:T(2,128)(2,1)} %copy.103) | data formatting | bytes 6291456 | tf_op jit(solution)/shard_map/reshape | solution.py:15
  32.4 3.2 fusion.20
  36.5 0.8 copy.109
  37.2 14.4 %all-to-all-start.1 = ((bf16[1,96,256,2]{1,3,0,2:T(2,128)(2,1)}), bf16[1,96,256,2]{1,3,0,2:T(2,128)(2,1)S(1)}, u32[]{:S(2)}, u32[]{:S(2)}) async-start(bf16[1,96,256,2]{1,3,0,2:T(2,128)(2,1)} %copy.109), calls=%async_computation.1 | async-start | bytes 262144 | tf_op jit(solution)/shard_map/all_to_all | solution.py:82
  51.8 0.8 copy.106
  52.6 10.4 %all-to-all-done.1 = bf16[1,96,256,2]{1,3,0,2:T(2,128)(2,1)S(1)} async-done(((bf16[1,96,256,2]{1,3,0,2:T(2,128)(2,1)}), bf16[1,96,256,2]{1,3,0,2:T(2,128)(2,1)S(1)}, u32[]{:S(2)}, u32[]{:S(2)}) %all-to-all-start.1) | async-done | bytes 98336 | tf_op jit(solution)/shard_map/all_to_all | solution.py:82
  63.0 3.7 %all-to-all-start = ((bf16[1,96,256,2]{1,3,0,2:T(2,128)(2,1)}), bf16[1,96,256,2]{1,3,0,2:T(2,128)(2,1)S(1)}, u32[]{:S(2)}, u32[]{:S(2)}) async-start(bf16[1,96,256,2]{1,3,0,2:T(2,128)(2,1)} %copy.106), calls=%async_computation | async-start | bytes 262144 | tf_op jit(solution)/shard_map/all_to_all | solution.py:79
  66.7 2.9 copy.112
  69.6 8.2 %all-to-all-done = bf16[1,96,256,2]{1,3,0,2:T(2,128)(2,1)S(1)} async-done(((bf16[1,96,256,2]{1,3,0,2:T(2,128)(2,1)}), bf16[1,96,256,2]{1,3,0,2:T(2,128)(2,1)S(1)}, u32[]{:S(2)}, u32[]{:S(2)}) %all-to-all-start) | async-done | bytes 98336 | tf_op jit(solution)/shard_map/all_to_all | solution.py:79
  77.8 7.2 %all-to-all-start.3 = ((bf16[8,96,1024]{1,0,2:T(8,128)(2,1)}), bf16[8,96,1024]{1,0,2:T(8,128)(2,1)S(1)}, u32[]{:S(2)}, u32[]{:S(2)}) async-start(bf16[8,96,1024]{1,0,2:T(8,128)(2,1)} %copy.112), calls=%async_computation.3 | async-start | bytes 4194304 | tf_op jit(solution)/shard_map/all_to_all | solution.py:86
  85.2 48.4 %all-to-all-done.3 = bf16[8,96,1024]{1,0,2:T(8,128)(2,1)S(1)} async-done(((bf16[8,96,1024]{1,0,2:T(8,128)(2,1)}), bf16[8,96,1024]{1,0,2:T(8,128)(2,1)S(1)}, u32[]{:S(2)}, u32[]{:S(2)}) %all-to-all-start.3) | async-done | bytes 1572896 | tf_op jit(solution)/shard_map/all_to_all | solution.py:86
  133.6 3.0 stack.8
  136.6 6.7 %all-to-all-start.2 = ((bf16[16,32,2,96,8,2]{3,1,5,2,4,0:T(8,128)(2,1)}), bf16[16,32,2,96,8,2]{3,1,5,2,4,0:T(8,128)(2,1)}, u32[]{:S(2)}, u32[]{:S(2)}) async-start(bf16[16,32,2,96,8,2]{3,1,5,2,4,0:T(8,128)(2,1)} %stack.8), calls=%async_computation.2 | async-start | bytes 8388608 | tf_op jit(solution)/shard_map/all_to_all | solution.py:88
  143.6 2.0 copy.102
  145.6 1.4 copy.115
  147.5 2.3 fusion.23
  149.8 88.2 %all-to-all-done.2 = bf16[16,32,2,96,8,2]{3,1,5,2,4,0:T(8,128)(2,1)} async-done(((bf16[16,32,2,96,8,2]{3,1,5,2,4,0:T(8,128)(2,1)}), bf16[16,32,2,96,8,2]{3,1,5,2,4,0:T(8,128)(2,1)}, u32[]{:S(2)}, u32[]{:S(2)}) %all-to-all-start.2) | async-done | bytes 3145760 | tf_op jit(solution)/shard_map/all_to_all | solution.py:88
  238.1 3.4 %convert_bitcast_fusion = bf16[16,64,8,2,2,32]{1,5,4,3,2,0:T(8,128)(2,1)S(1)} fusion(bf16[16,32,2,96,8,2]{3,1,5,2,4,0:T(8,128)(2,1)} %all-to-all-done.2, bf16[8,96,16,64]{1,0,3,2:T(8,128)(2,1)S(1)} %bitcast.99), kind=kOutput, calls=%fused_computation.24 | convolution fusion | flops 202375168 | bytes 6815744 | tf_op jit(solution)/shard_map/obtl,rfbtok->blofkr/dot_general | solution.py:96
  241.5 1.0 convert_reduce_fusion
  242.9 1.1 add_bitcast_fusion
  244.0 0.9 broadcast.273.clone2
  244.8 78.2 %while.30 = (s32[]{:T(128)}, f32[64,8,4]{1,2,0:T(4,128)S(1)}, f32[4,64,8,4,8]{1,4,3,2,0:T(8,128)}, f32[4,64,8,4,8]{1,4,0,3,2:T(8,128)}, f32[4]{0:T(128)S(1)}, /*index=5*/f32[4,64,8,8]{3,2,1,0:T(8,128)}, s32[]{:T(128)}) while((s32[]{:T(128)}, f32[64,8,4]{1,2,0:T(4,128)S(1)}, f32[4,64,8,4,8]{1,4,3,2,0:T(8,128)}, ...), condition=%wide.region_3.4_spmd.clone, body=%wide.region_2.3_spmd.clone.sunk | while | flops 1607698 | bytes 1025185 | solution.py:58
  245.0 0.9 constant_dynamic-slice_fusion.5
  246.0 0.9 copy.149
  248.2 14.9 %fusion.30 = f32[64,8,4,8]{1,3,2,0:T(8,128)S(1)} fusion(f32[1,64,8,4,8]{4,2,3,1,0:T(8,128)S(1)} %copy.149, f32[8]{0:T(128)S(1)} %compare_convert_fusion.2, f32[64,8,4]{1,2,0:T(4,128)S(1)} %bitcast.106, f32[4,64,8,8]{3,2,1,0:T(8,128)} %get-tuple-element.387, s32[]{:T(128)} %get-tuple-element.375), kind=kOutput, calls=%fused_computation.9.clone.1 | convolution fusion | flops 1605632 | bytes 401952 | tf_op jit(solution)/shard_map/while/body/eval_jaxpr/lij,locj->loci/dot_general | solution.py:48
  263.7 0.7 constant_dynamic-update-slice_fusion.2
  264.5 0.9 constant_dynamic-slice_fusion.5
  265.5 0.9 copy.149
  267.7 14.9 %fusion.30 = f32[64,8,4,8]{1,3,2,0:T(8,128)S(1)} fusion(f32[1,64,8,4,8]{4,2,3,1,0:T(8,128)S(1)} %copy.149, f32[8]{0:T(128)S(1)} %compare_convert_fusion.2, f32[64,8,4]{1,2,0:T(4,128)S(1)} %bitcast.106, f32[4,64,8,8]{3,2,1,0:T(8,128)} %get-tuple-element.387, s32[]{:T(128)} %get-tuple-element.375), kind=kOutput, calls=%fused_computation.9.clone.1 | convolution fusion | flops 1605632 | bytes 401952 | tf_op jit(solution)/shard_map/while/body/eval_jaxpr/lij,locj->loci/dot_general | solution.py:48
  283.2 0.7 constant_dynamic-update-slice_fusion.2
  284.0 0.9 constant_dynamic-slice_fusion.5
  285.0 0.9 copy.149
  285.9 0.6 dynamic_slice.66
  287.2 14.9 %fusion.30 = f32[64,8,4,8]{1,3,2,0:T(8,128)S(1)} fusion(f32[1,64,8,4,8]{4,2,3,1,0:T(8,128)S(1)} %copy.149, f32[8]{0:T(128)S(1)} %compare_convert_fusion.2, f32[64,8,4]{1,2,0:T(4,128)S(1)} %bitcast.106, f32[4,64,8,8]{3,2,1,0:T(8,128)} %get-tuple-element.387, s32[]{:T(128)} %get-tuple-element.375), kind=kOutput, calls=%fused_computation.9.clone.1 | convolution fusion | flops 1605632 | bytes 401952 | tf_op jit(solution)/shard_map/while/body/eval_jaxpr/lij,locj->loci/dot_general | solution.py:48
  302.7 0.7 constant_dynamic-update-slice_fusion.2
  303.5 0.9 constant_dynamic-slice_fusion.5
  304.4 0.9 copy.149
  306.7 14.9 %fusion.30 = f32[64,8,4,8]{1,3,2,0:T(8,128)S(1)} fusion(f32[1,64,8,4,8]{4,2,3,1,0:T(8,128)S(1)} %copy.149, f32[8]{0:T(128)S(1)} %compare_convert_fusion.2, f32[64,8,4]{1,2,0:T(4,128)S(1)} %bitcast.106, f32[4,64,8,8]{3,2,1,0:T(8,128)} %get-tuple-element.387, s32[]{:T(128)} %get-tuple-element.375), kind=kOutput, calls=%fused_computation.9.clone.1 | convolution fusion | flops 1605632 | bytes 401952 | tf_op jit(solution)/shard_map/while/body/eval_jaxpr/lij,locj->loci/dot_general | solution.py:48
  322.2 0.7 constant_dynamic-update-slice_fusion.2
  323.1 9.2 %while.29 = (s32[]{:T(128)}, f32[64,8,4]{0,2,1:T(4,128)S(1)}, f32[4,64,8,4,8]{1,4,3,2,0:T(8,128)S(1)}, f32[4,64,8,4,8]{1,4,3,2,0:T(8,128)}, f32[4]{0:T(128)S(1)}...) while((s32[]{:T(128)}, f32[64,8,4]{0,2,1:T(4,128)S(1)}, f32[4,64,8,4,8]{1,4,3,2,0:T(8,128)S(1)}, ...), condition=%wide.region_5.6_spmd, body=%wide.region_4.5_spmd.sunk | while | flops 38915 | bytes 459641 | solution.py:59
  324.4 0.9 subtract_dynamic-update-slice_fusion.2
  326.7 0.9 subtract_dynamic-update-slice_fusion.2
  329.0 0.9 subtract_dynamic-update-slice_fusion.2
  331.3 0.9 subtract_dynamic-update-slice_fusion.2
  332.3 0.9 copy.122
  (90 shorter events, 14.9 us)
Async XLA Ops:
  0.0 32.4 %copy-start = (bf16[1,2,96,3072]{3,2,1,0:T(8,128)(2,1)S(1)}, bf16[1,2,96,3072]{3,2,1,0:T(8,128)(2,1)}, u32[]{:S(2)}) copy-start(bf16[1,2,96,3072]{3,2,1,0:T(8,128)(2,1)} %param.10) | copy-start | bytes 3538948
  32.4 34.3 %copy-start.4 = (bf16[8,96,1024]{2,1,0:T(8,128)(2,1)S(1)}, bf16[8,96,1024]{2,1,0:T(8,128)(2,1)}, u32[]{:S(2)}) copy-start(bf16[8,96,1024]{2,1,0:T(8,128)(2,1)} %param.11) | copy-start | bytes 4718596
  37.2 25.8 %all-to-all-start.1 = ((bf16[1,96,256,2]{1,3,0,2:T(2,128)(2,1)}), bf16[1,96,256,2]{1,3,0,2:T(2,128)(2,1)S(1)}, u32[]{:S(2)}, u32[]{:S(2)}) async-start(bf16[1,96,256,2]{1,3,0,2:T(2,128)(2,1)} %copy.109), calls=%async_computation.1 | async-start | bytes 262144 | tf_op jit(solution)/shard_map/all_to_all | solution.py:82
  63.0 14.8 %all-to-all-start = ((bf16[1,96,256,2]{1,3,0,2:T(2,128)(2,1)}), bf16[1,96,256,2]{1,3,0,2:T(2,128)(2,1)S(1)}, u32[]{:S(2)}, u32[]{:S(2)}) async-start(bf16[1,96,256,2]{1,3,0,2:T(2,128)(2,1)} %copy.106), calls=%async_computation | async-start | bytes 262144 | tf_op jit(solution)/shard_map/all_to_all | solution.py:79
  77.8 55.7 %all-to-all-start.3 = ((bf16[8,96,1024]{1,0,2:T(8,128)(2,1)}), bf16[8,96,1024]{1,0,2:T(8,128)(2,1)S(1)}, u32[]{:S(2)}, u32[]{:S(2)}) async-start(bf16[8,96,1024]{1,0,2:T(8,128)(2,1)} %copy.112), calls=%async_computation.3 | async-start | bytes 4194304 | tf_op jit(solution)/shard_map/all_to_all | solution.py:86
  136.6 6.9 %copy-start.6 = (s32[256]{0:T(256)S(1)}, s32[256]{0:T(256)}, u32[]{:S(2)}) copy-start(s32[256]{0:T(256)} %param.12) | copy-start | bytes 3076
  136.6 8.9 %copy-start.5 = (f32[64,4,8,8]{0,3,2,1:T(8,128)S(1)}, f32[64,4,8,8]{0,3,2,1:T(8,128)}, u32[]{:S(2)}) copy-start(f32[64,4,8,8]{0,3,2,1:T(8,128)} %param.15) | copy-start | bytes 196612
  136.6 10.4 %copy-start.7 = (s32[256]{0:T(256)S(1)}, s32[256]{0:T(256)}, u32[]{:S(2)}) copy-start(s32[256]{0:T(256)} %param.13) | copy-start | bytes 3076
  136.6 101.4 %all-to-all-start.2 = ((bf16[16,32,2,96,8,2]{3,1,5,2,4,0:T(8,128)(2,1)}), bf16[16,32,2,96,8,2]{3,1,5,2,4,0:T(8,128)(2,1)}, u32[]{:S(2)}, u32[]{:S(2)}) async-start(bf16[16,32,2,96,8,2]{3,1,5,2,4,0:T(8,128)(2,1)} %stack.8), calls=%async_computation.2 | async-start | bytes 8388608 | tf_op jit(solution)/shard_map/all_to_all | solution.py:88
  241.5 1.0 copy-start.1
  241.5 1.2 copy-start.2
  241.5 1.3 copy-start.3
